TPU v7x, 32 devices: a whole 2x2x4 slice. The times are simulated.
32 devices in a mesh: dp: 16 (over z, x, core), seq: 2 (over y).
Axes of the slice: x: 2, y: 2, z: 4, core: 2. Of those that a mesh axis runs over, the one named last changes fastest.
Arguments:
- tokens: bfloat16 [16384, 1024], P(('dp', 'seq')), may hold values from -6 to 6
- lengths: int32 [16, 3], P('dp'), may hold values from 1 to 512, 1024 in all within a row
- attn_gain: float32 [1024], replicated, may hold values from 0.25 to 1.75
- attn_shift: float32 [1024], replicated, may hold values from -1.5 to 1.5
- w_qkv: bfloat16 [1024, 3072], P('dp'), may hold values from -0.1875 to 0.1875
- w_out: bfloat16 [1024, 1024], P('dp'), may hold values from -0.5 to 0.5
- ffn_gain: float32 [1024], replicated, may hold values from 0.25 to 1.75
- ffn_shift: float32 [1024], replicated, may hold values from -1.5 to 1.5
- w_up: bfloat16 [1024, 4096], P('dp'), may hold values from -0.1875 to 0.1875
- b_up: float32 [4096], replicated, may hold values from -2.5 to 2.5
- w_down: bfloat16 [4096, 1024], P('dp'), may hold values from -0.125 to 0.125
- b_down: float32 [1024], replicated, may hold values from -2.5 to 2.5
- cotangent: bfloat16 [16384, 1024], P(('dp', 'seq')), may hold values from -6 to 6
Outputs:
- block_out: bfloat16 [16384, 1024], P(('dp', 'seq'))
- grad_tokens: bfloat16 [16384, 1024], P(('dp', 'seq'))
- grad_attn_gain: float32 [1024], replicated
- grad_attn_shift: float32 [1024], replicated
- grad_w_qkv: float32 [1024, 3072], replicated
- grad_w_out: float32 [1024, 1024], replicated
- grad_ffn_gain: float32 [1024], replicated
- grad_ffn_shift: float32 [1024], replicated
- grad_w_up: float32 [1024, 4096], replicated
- grad_b_up: float32 [4096], replicated
- grad_w_down: float32 [4096, 1024], replicated
- grad_b_down: float32 [1024], replicated
Inputs may be any that keep to these rules, and one draw needn't show every extreme that they name: Each row of lengths sums to 1024.
All inputs are finite; a program needn't handle non-finite values.
Results may differ from a plain program's by a relative error of at most 0.02.
Values may be sent and summed in bfloat16 or wider, within the bound.
A program may use at most 256 MiB of HBM per device.

v0:
```python
import jax
import jax.numpy as jnp
from jax import lax
from jax.sharding import PartitionSpec as P

HEADS = 8


EPS = 1e-05


def inner_rows(left, right):
    return lax.dot_general(
        left, right, (((0,), (0,)), ((), ())), preferred_element_type=jnp.float32
    )


def times_transposed(left, right):
    return lax.dot_general(
        left, right, (((1,), (1,)), ((), ())), preferred_element_type=jnp.float32
    )


def smooth_act(values):
    return jax.nn.gelu(values, approximate=True)


def norm_forward(values, gain, shift):
    mean = jnp.mean(values, axis=-1, keepdims=True)
    centred = values - mean
    variance = jnp.mean(centred * centred, axis=-1, keepdims=True)
    factor = lax.rsqrt(variance + EPS)
    normed = centred * factor
    return (normed * gain + shift, normed, factor)


def norm_backward(grad_out, normed, factor, gain):
    grad_normed = grad_out * gain
    centre_term = jnp.mean(grad_normed, axis=-1, keepdims=True)
    along_term = jnp.mean(grad_normed * normed, axis=-1, keepdims=True)
    grad_in = factor * (grad_normed - centre_term - normed * along_term)
    return (grad_in, jnp.sum(grad_out * normed, axis=0), jnp.sum(grad_out, axis=0))


def item_ids(item_lengths, count):
    item_ends = jnp.cumsum(item_lengths, dtype=jnp.int32)
    places = jnp.arange(count, dtype=jnp.int32)
    hits = (places[:, None] >= item_ends[None, :]).astype(jnp.int32)
    return jnp.sum(hits, axis=1, dtype=jnp.int32)


def block_scores(query_block, keys, start, item_of, slopes):
    rows = query_block.shape[0]
    count = keys.shape[0]
    scale = query_block.shape[-1] ** (-0.5)
    raw = jnp.einsum("qhd,khd->hqk", query_block, keys, preferred_element_type=jnp.float32)
    row_places = start + jnp.arange(rows, dtype=jnp.int32)
    col_places = jnp.arange(count, dtype=jnp.int32)
    distance = (row_places[:, None] - col_places[None, :]).astype(jnp.float32)
    row_items = lax.dynamic_slice_in_dim(item_of, start, rows)
    allowed = (row_items[:, None] == item_of[None, :]) & (
        col_places[None, :] <= row_places[:, None]
    )
    scores = raw * scale - slopes[:, None, None] * distance[None]
    return jnp.where(allowed[None], scores, jnp.float32(-1000000000.0))


def attend(heads_qkv, item_of, slopes):
    count = heads_qkv.shape[0]
    rows = min(512, count)
    queries = heads_qkv[:, 0]
    keys = heads_qkv[:, 1]
    values = heads_qkv[:, 2]

    def one_block(index):
        start = index * rows
        query_block = lax.dynamic_slice_in_dim(queries, start, rows)
        scores = block_scores(query_block, keys, start, item_of, slopes)
        top = jnp.max(scores, axis=-1, keepdims=True)
        weights = jnp.exp(scores - top)
        total = jnp.sum(weights, axis=-1, keepdims=True)
        probs = (weights / total).astype(jnp.bfloat16)
        mixed = jnp.einsum("hqk,khd->qhd", probs, values, preferred_element_type=jnp.float32)
        return (mixed.astype(jnp.bfloat16), (top + jnp.log(total))[..., 0])

    mixed, log_norm = lax.map(one_block, jnp.arange(count // rows, dtype=jnp.int32))
    return (mixed.reshape(count, mixed.shape[2], mixed.shape[3]), log_norm)


def attend_back(heads_qkv, heads_out, grad_heads, log_norm, item_of, slopes):
    count = heads_qkv.shape[0]
    rows = min(512, count)
    queries = heads_qkv[:, 0]
    keys = heads_qkv[:, 1]
    values = heads_qkv[:, 2]
    scale = queries.shape[-1] ** (-0.5)
    row_dots = jnp.sum(grad_heads.astype(jnp.float32) * heads_out.astype(jnp.float32), axis=-1)

    def one_block(carry, index):
        grad_keys, grad_values = carry
        start = index * rows
        query_block = lax.dynamic_slice_in_dim(queries, start, rows)
        grad_block = lax.dynamic_slice_in_dim(grad_heads, start, rows)
        dots = lax.dynamic_slice_in_dim(row_dots, start, rows)
        scores = block_scores(query_block, keys, start, item_of, slopes)
        probs = jnp.exp(scores - log_norm[index][:, :, None])
        probs_low = probs.astype(jnp.bfloat16)
        grad_values = grad_values + jnp.einsum(
            "hqk,qhd->khd", probs_low, grad_block, preferred_element_type=jnp.float32
        )
        grad_probs = jnp.einsum(
            "qhd,khd->hqk", grad_block, values, preferred_element_type=jnp.float32
        )
        grad_scores = (probs * (grad_probs - jnp.transpose(dots)[:, :, None])).astype(jnp.bfloat16)
        grad_query = (
            jnp.einsum("hqk,khd->qhd", grad_scores, keys, preferred_element_type=jnp.float32)
            * scale
        )
        grad_keys = (
            grad_keys
            + jnp.einsum(
                "hqk,qhd->khd", grad_scores, query_block, preferred_element_type=jnp.float32
            )
            * scale
        )
        return ((grad_keys, grad_values), grad_query)

    empty = jnp.zeros(keys.shape, jnp.float32)
    (grad_keys, grad_values), grad_query = lax.scan(
        one_block, (empty, empty), jnp.arange(count // rows, dtype=jnp.int32)
    )
    grad_query = grad_query.reshape(keys.shape)
    return jnp.stack([grad_query, grad_keys, grad_values], axis=1).astype(jnp.bfloat16)


def on_device(
    tokens,
    lengths,
    attn_gain,
    attn_shift,
    w_qkv,
    w_out,
    ffn_gain,
    ffn_shift,
    w_up,
    b_up,
    w_down,
    b_down,
    cotangent,
):
    w_qkv, w_out, w_up, w_down = (
        lax.all_gather(w_qkv, "dp", axis=0, tiled=True),
        lax.all_gather(w_out, "dp", axis=0, tiled=True),
        lax.all_gather(w_up, "dp", axis=0, tiled=True),
        lax.all_gather(w_down, "dp", axis=0, tiled=True),
    )
    local, width = tokens.shape
    groups = lax.axis_size("seq")
    per_head = width // HEADS
    local_heads = HEADS // groups
    count = local * groups
    item_of = item_ids(lengths[0], count)
    first_head = lax.axis_index("seq") * local_heads
    exponents = (first_head + jnp.arange(local_heads, dtype=jnp.int32) + 1).astype(jnp.float32)
    slopes = jnp.exp2(-exponents)
    inputs = tokens.astype(jnp.float32)
    normed_in, unit_in, factor_in = norm_forward(inputs, attn_gain, attn_shift)
    first_in = normed_in.astype(jnp.bfloat16)
    projected = jnp.dot(first_in, w_qkv, preferred_element_type=jnp.float32).astype(jnp.bfloat16)
    projected = projected.reshape(local, 3, HEADS, per_head)
    heads_qkv = lax.all_to_all(projected, "seq", split_axis=2, concat_axis=0, tiled=True)
    heads_out, log_norm = attend(heads_qkv, item_of, slopes)
    joined = lax.all_to_all(heads_out, "seq", split_axis=0, concat_axis=1, tiled=True).reshape(
        local, width
    )
    middle = inputs + jnp.dot(joined, w_out, preferred_element_type=jnp.float32)
    normed_mid, unit_mid, factor_mid = norm_forward(middle, ffn_gain, ffn_shift)
    second_in = normed_mid.astype(jnp.bfloat16)
    pre_act = jnp.dot(second_in, w_up, preferred_element_type=jnp.float32) + b_up
    act_value, act_pull = jax.vjp(smooth_act, pre_act)
    active = act_value.astype(jnp.bfloat16)
    block_out = (
        middle + jnp.dot(active, w_down, preferred_element_type=jnp.float32) + b_down
    ).astype(jnp.bfloat16)
    grad_out = cotangent.astype(jnp.float32)
    grad_b_down = jnp.sum(grad_out, axis=0)
    grad_w_down = inner_rows(active, cotangent)
    grad_active = times_transposed(cotangent, w_down)
    grad_pre = act_pull(grad_active)[0]
    grad_b_up = jnp.sum(grad_pre, axis=0)
    grad_pre_low = grad_pre.astype(jnp.bfloat16)
    grad_w_up = inner_rows(second_in, grad_pre_low)
    grad_second = times_transposed(grad_pre_low, w_up)
    grad_mid_norm, grad_ffn_gain, grad_ffn_shift = norm_backward(
        grad_second, unit_mid, factor_mid, ffn_gain
    )
    grad_middle = grad_out + grad_mid_norm
    grad_branch = grad_middle.astype(jnp.bfloat16)
    grad_w_out = inner_rows(joined, grad_branch)
    grad_joined = (
        times_transposed(grad_branch, w_out).astype(jnp.bfloat16).reshape(local, HEADS, per_head)
    )
    grad_heads = lax.all_to_all(grad_joined, "seq", split_axis=1, concat_axis=0, tiled=True)
    grad_qkv_heads = attend_back(heads_qkv, heads_out, grad_heads, log_norm, item_of, slopes)
    grad_projected = lax.all_to_all(
        grad_qkv_heads, "seq", split_axis=0, concat_axis=2, tiled=True
    ).reshape(local, 3 * width)
    grad_w_qkv = inner_rows(first_in, grad_projected)
    grad_first = times_transposed(grad_projected, w_qkv)
    grad_in_norm, grad_attn_gain, grad_attn_shift = norm_backward(
        grad_first, unit_in, factor_in, attn_gain
    )
    grad_tokens = (grad_middle + grad_in_norm).astype(jnp.bfloat16)
    all_part = (
        lax.psum_scatter(
            grad_attn_gain.astype(jnp.bfloat16), "dp", scatter_dimension=0, tiled=True
        ).astype(jnp.float32),
        lax.psum_scatter(
            grad_attn_shift.astype(jnp.bfloat16), "dp", scatter_dimension=0, tiled=True
        ).astype(jnp.float32),
        lax.psum_scatter(
            grad_w_qkv.astype(jnp.bfloat16), "dp", scatter_dimension=0, tiled=True
        ).astype(jnp.float32),
        lax.psum_scatter(
            grad_w_out.astype(jnp.bfloat16), "dp", scatter_dimension=0, tiled=True
        ).astype(jnp.float32),
        lax.psum_scatter(
            grad_ffn_gain.astype(jnp.bfloat16), "dp", scatter_dimension=0, tiled=True
        ).astype(jnp.float32),
        lax.psum_scatter(
            grad_ffn_shift.astype(jnp.bfloat16), "dp", scatter_dimension=0, tiled=True
        ).astype(jnp.float32),
        lax.psum_scatter(
            grad_w_up.astype(jnp.bfloat16), "dp", scatter_dimension=0, tiled=True
        ).astype(jnp.float32),
        lax.psum_scatter(
            grad_b_up.astype(jnp.bfloat16), "dp", scatter_dimension=0, tiled=True
        ).astype(jnp.float32),
        lax.psum_scatter(
            grad_w_down.astype(jnp.bfloat16), "dp", scatter_dimension=0, tiled=True
        ).astype(jnp.float32),
        lax.psum_scatter(
            grad_b_down.astype(jnp.bfloat16), "dp", scatter_dimension=0, tiled=True
        ).astype(jnp.float32),
    )
    all_part = (
        lax.psum(all_part[0].astype(jnp.bfloat16), "seq").astype(jnp.float32),
        lax.psum(all_part[1].astype(jnp.bfloat16), "seq").astype(jnp.float32),
        lax.psum(all_part[2].astype(jnp.bfloat16), "seq").astype(jnp.float32),
        lax.psum(all_part[3].astype(jnp.bfloat16), "seq").astype(jnp.float32),
        lax.psum(all_part[4].astype(jnp.bfloat16), "seq").astype(jnp.float32),
        lax.psum(all_part[5].astype(jnp.bfloat16), "seq").astype(jnp.float32),
        lax.psum(all_part[6].astype(jnp.bfloat16), "seq").astype(jnp.float32),
        lax.psum(all_part[7].astype(jnp.bfloat16), "seq").astype(jnp.float32),
        lax.psum(all_part[8].astype(jnp.bfloat16), "seq").astype(jnp.float32),
        lax.psum(all_part[9].astype(jnp.bfloat16), "seq").astype(jnp.float32),
    )
    summed = (
        lax.all_gather(all_part[0].astype(jnp.bfloat16), "dp", axis=0, tiled=True).astype(
            jnp.float32
        ),
        lax.all_gather(all_part[1].astype(jnp.bfloat16), "dp", axis=0, tiled=True).astype(
            jnp.float32
        ),
        lax.all_gather(all_part[2].astype(jnp.bfloat16), "dp", axis=0, tiled=True).astype(
            jnp.float32
        ),
        lax.all_gather(all_part[3].astype(jnp.bfloat16), "dp", axis=0, tiled=True).astype(
            jnp.float32
        ),
        lax.all_gather(all_part[4].astype(jnp.bfloat16), "dp", axis=0, tiled=True).astype(
            jnp.float32
        ),
        lax.all_gather(all_part[5].astype(jnp.bfloat16), "dp", axis=0, tiled=True).astype(
            jnp.float32
        ),
        lax.all_gather(all_part[6].astype(jnp.bfloat16), "dp", axis=0, tiled=True).astype(
            jnp.float32
        ),
        lax.all_gather(all_part[7].astype(jnp.bfloat16), "dp", axis=0, tiled=True).astype(
            jnp.float32
        ),
        lax.all_gather(all_part[8].astype(jnp.bfloat16), "dp", axis=0, tiled=True).astype(
            jnp.float32
        ),
        lax.all_gather(all_part[9].astype(jnp.bfloat16), "dp", axis=0, tiled=True).astype(
            jnp.float32
        ),
    )
    return (
        block_out,
        grad_tokens,
        summed[0],
        summed[1],
        summed[2],
        summed[3],
        summed[4],
        summed[5],
        summed[6],
        summed[7],
        summed[8],
        summed[9],
    )


def solution(mesh):
    return jax.shard_map(
        on_device,
        mesh=mesh,
        in_specs=(
            P(("dp", "seq"), None),
            P("dp", None),
            P(),
            P(),
            P("dp", None),
            P("dp", None),
            P(),
            P(),
            P("dp", None),
            P(),
            P("dp", None),
            P(),
            P(("dp", "seq"), None),
        ),
        out_specs=(
            P(("dp", "seq"), None),
            P(("dp", "seq"), None),
            P(),
            P(),
            P(),
            P(),
            P(),
            P(),
            P(),
            P(),
            P(),
            P(),
        ),
        check_vma=False,
    )
```

profile of v0, /device:TPU:17, one launch (start us, length us, event | category | flops | bytes accessed | tf_op | source)
XLA Modules:
  0.0 1072.4 jit_solution(3538946769971904313)
XLA Ops:
  11.9 61.3 %all-gather.10.cloned.1.call-done = bf16[1024,3072]{1,0:T(8,128)(2,1)} async-done(((bf16[64,3072]{1,0:T(8,128)(2,1)}), bf16[1024,3072]{1,0:T(8,128)(2,1)}) %all-gather.10.cloned.1.call-update) | async-done | bytes 6291472 | tf_op jit(solution)/shard_map/all_gather | solution.py:152
  73.2 6.7 fusion.60
  83.2 5.4 all-to-all-start
  88.9 35.8 %all-to-all-done = bf16[512,3,8,128]{3,0,1,2:T(8,128)(2,1)} async-done(((bf16[512,3,8,128]{3,0,1,2:T(8,128)(2,1)}), bf16[512,3,8,128]{3,0,1,2:T(8,128)(2,1)}, u32[]{:S(2)}, u32[]{:S(2)}) %all-to-all-start) | async-done | bytes 3145760 | tf_op jit(solution)/shard_map/all_to_all | solution.py:171
  128.5 28.2 %while.28 = (s32[]{:T(128)}, bf16[2,512,4,128]{3,1,2,0:T(8,128)(2,1)}, f32[2,4,512]{2,1,0:T(4,128)S(1)}, s32[2]{0:T(128)S(1)}, s32[1024]{0:T(1024)S(1)}, /*index...) while((s32[]{:T(128)}, ...), condition=%wide.region_7.8_spmd.clone, body=%wide.region_4.7_spmd.clone.sunk | while | flops 1114372608 | bytes 51463004 | solution.py:86
  130.7 3.7 fusion.116
  137.5 4.2 fusion.118
  144.8 3.7 fusion.116
  151.6 4.2 fusion.118
  158.9 15.6 %all_to_all.66 = bf16[1024,4,128]{2,1,0:T(4,128)(2,1)S(1)} all-to-all(bf16[1024,4,128]{2,1,0:T(4,128)(2,1)S(1)} %copy.90), channel_id=1, replica_groups=mesh['dp'=16,'seq'=2] {'seq'}, dimensions={0} | all-to-all | bytes 2097152 | tf_op jit(solution)/shard_map/all_to_all | solution.py:173
  179.9 11.1 %all-gather.14.cloned.1.call-done = bf16[1024,4096]{1,0:T(8,128)(2,1)} async-done(((bf16[64,4096]{1,0:T(8,128)(2,1)}), bf16[1024,4096]{1,0:T(8,128)(2,1)}) %all-gather.14.cloned.1.call-update) | async-done | bytes 8388624 | tf_op jit(solution)/shard_map/all_gather | solution.py:154
  191.0 10.3 fusion.66
  201.3 64.8 %all-gather.16.cloned.1.call-done = bf16[4096,1024]{1,0:T(8,128)(2,1)} async-done(((bf16[256,1024]{1,0:T(8,128)(2,1)}), bf16[4096,1024]{1,0:T(8,128)(2,1)}) %all-gather.16.cloned.1.call-update) | async-done | bytes 8388624 | tf_op jit(solution)/shard_map/all_gather | solution.py:155
  266.1 15.3 %fusion.67 = (bf16[4096]{0:T(1024)(128)(2,1)}, bf16[512,4096]{1,0:T(8,128)(2,1)}) fusion(f32[512,4096]{1,0:T(8,128)} %fusion.66, f32[4096]{0:T(1024)S(1)} %copy-done.34, bf16[512,1024]{1,0:T(8,128)(2,1)} %param.29, bf16[4096,1024]{1,0:T(8,128)(2,1)} %all-gather.16.cloned.1.call-done), kind=kOutput, calls=%fused_computation.118 | convolution fusion | flops 4341100544 | bytes 22044672 | tf_op jit(solution)/shard_map/dot_general | solution.py:19
  281.5 7.7 multiply_reduce_fusion
  293.2 4.4 all-to-all-start.2
  297.7 4.5 convolution_convert_fusion.4
  302.3 8.9 all-to-all-done.2
  315.9 62.0 %while.29 = (s32[]{:T(128)}, f32[1024,4,128]{0,2,1:T(8,128)S(1)}, f32[1024,4,128]{0,2,1:T(8,128)}, bf16[2,512,4,128]{3,1,0,2:T(8,128)(2,1)}, s32[2]{0:T(128)S(1)...) while((s32[]{:T(128)}, f32[1024,4,128]{0,2,1:T(8,128)S(1)}, ...), condition=%wide.region_14.15_spmd.clone, body=%wide.region_13.14_spmd.clone.sunk | while | flops 2719220224 | bytes 127476864 | solution.py:129
  317.3 5.7 fusion.129
  326.7 7.7 multiply_convert_fusion.5
  334.4 3.8 bitcast_add_fusion.4
  338.4 6.1 bitcast_add_fusion.5
  348.2 5.7 fusion.129
  357.6 7.7 multiply_convert_fusion.5
  365.3 3.8 bitcast_add_fusion.4
  369.4 6.0 bitcast_add_fusion.5
  385.4 37.9 %all_to_all.67 = bf16[1024,3,4,128]{3,2,1,0:T(4,128)(2,1)S(1)} all-to-all(bf16[1024,3,4,128]{3,2,1,0:T(4,128)(2,1)S(1)} %copy.98), channel_id=1, replica_groups=mesh['dp'=16,'seq'=2] {'seq'}, dimensions={0} | all-to-all | bytes 6291456 | tf_op jit(solution)/shard_map/all_to_all | solution.py:205
  425.5 4.8 copy.100
  430.3 7.8 convolution_convert_fusion.2
  439.7 9.2 convolution_convert_fusion.1
  449.0 14.1 %convolution_convert_fusion = bf16[4096,1024]{1,0:T(8,128)(2,1)} fusion(bf16[512,1024]{1,0:T(8,128)(2,1)} %param.29, f32[512,4096]{1,0:T(8,128)} %fusion.66, f32[4096]{0:T(1024)S(1)} %copy-done.34), kind=kOutput, calls=%fused_computation.59 | convolution fusion | flops 4320133120 | bytes 17842176 | tf_op jit(solution)/shard_map/dot_general | solution.py:13
  463.2 58.5 %reduce-scatter.5.cloned.1.call-done = bf16[64,3072]{1,0:T(8,128)(2,1)} async-done(((bf16[1024,3072]{1,0:T(8,128)(2,1)}), bf16[64,3072]{1,0:T(8,128)(2,1)}) %reduce-scatter.5.cloned.1.call-update) | async-done | bytes 393232 | tf_op jit(solution)/shard_map/reduce_scatter | solution.py:221
  521.7 109.6 %reduce-scatter.9.cloned.1.call-done = bf16[64,4096]{1,0:T(8,128)(2,1)} async-done(((bf16[1024,4096]{1,0:T(8,128)(2,1)}), bf16[64,4096]{1,0:T(8,128)(2,1)}) %reduce-scatter.9.cloned.1.call-update) | async-done | bytes 524304 | tf_op jit(solution)/shard_map/reduce_scatter | solution.py:233
  631.4 109.1 %reduce-scatter.11.cloned.1.call-done = bf16[256,1024]{1,0:T(8,128)(2,1)} async-done(((bf16[4096,1024]{1,0:T(8,128)(2,1)}), bf16[256,1024]{1,0:T(8,128)(2,1)}) %reduce-scatter.11.cloned.1.call-update) | async-done | bytes 524304 | tf_op jit(solution)/shard_map/reduce_scatter | solution.py:239
  740.6 54.4 %all-reduce.17.cloned.1.call-done = (bf16[64,3072]{1,0:T(8,128)(2,1)}, bf16[64,1024]{1,0:T(8,128)(2,1)}, bf16[64,4096]{1,0:T(8,128)(2,1)}, bf16[256,1024]{1,0:T(8,128)(2,1)}) async-done(((bf16[64,3072]{1,0:T(8,128)(2,1)}, bf16[64,1024]{1,0:T(8,128)(2,1)}, bf16[64,4096]{1,0:T(8,128)(2,1)}, bf16[256,1024]{1,0:T(8,128)(2,1)}), (bf16[64,3072]{1,0:T(8,128)(2,1)}, bf16[64,1024]{1,0:T(8,128)(2,1)}, ...) | async-done | bytes 1572880 | tf_op jit(solution)/shard_map/psum | solution.py:249
  801.1 12.5 %add_convert_fusion = bf16[512,1024]{1,0:T(8,128)(2,1)} fusion(f32[512,1024]{1,0:T(8,128)S(1)} %copy-done.4, bf16[4096,1024]{1,0:T(8,128)(2,1)} %all-gather.16.cloned.1.call-done, f32[1024]{0:T(1024)S(1)} %copy-done.39, f32[512,4096]{1,0:T(8,128)} %fusion.66, f32[4096]{0:T(1024)S(1)} %copy-done.34), kind=kOutput, calls=%fused_computation.89 | convolution fusion | flops 4317511680 | bytes 19943424 | tf_op jit(solution)/shard_map/dot_general | solution.py:183
  813.6 8.4 fusion.55
  822.0 47.2 %all-reduce.12 = (bf16[1024]{0:T(1024)(128)(2,1)S(1)}, bf16[1024]{0:T(1024)(128)(2,1)S(1)}, bf16[1024]{0:T(1024)(128)(2,1)S(1)}, bf16[1024]{0:T(1024)(128)(2,1)S(1)}, bf16[1024]{0:T(1024)(128)(2,1)S(1)}) all-reduce(bf16[1024]{0:T(1024)(128)(2,1)S(1)} %get-tuple-element.202, ...), channel_id=2, replica_groups=mesh['dp'=16,'seq'=2] {'dp'}, use_global_device_ids=true, to_apply=%region_18.19.clone | all-reduce | flops 5120 | bytes 20480
  869.6 4.2 all-reduce.13
  874.8 60.1 %all-reduce.11 = (bf16[1024]{0:T(1024)(128)(2,1)S(1)}, bf16[1024]{0:T(1024)(128)(2,1)S(1)}, bf16[1024]{0:T(1024)(128)(2,1)S(1)}, bf16[1024]{0:T(1024)(128)(2,1)S...) all-reduce(bf16[1024]{0:T(1024)(128)(2,1)S(1)} %dynamic-update-slic, ...), channel_id=1, replica_groups=mesh['dp'=16,'seq'=2] {'dp'}, use_global_device_ids=true, to_apply=%add | all-reduce | flops 9216 | bytes 36864
  937.4 4.2 psum.77
  941.5 28.0 %all-gather = bf16[16,1,256]{2,1,0:T(2,128)(2,1)S(1)} all-gather(bf16[1,1,256]{2,1,0:T(2,128)(2,1)S(1)} %reshape.305), channel_id=1, replica_groups=mesh['dp'=16,'seq'=2] {'dp'}, dimensions={0}, use_global_device_ids=true | all-gather | bytes 8704 | tf_op jit(solution)/shard_map/all_gather | solution.py:280
  974.1 4.1 convert_element_type.197
  978.1 9.2 convert_element_type.195
  987.4 12.1 %convert_element_type.203 = f32[1024,4096]{1,0:T(8,128)} convert(bf16[1024,4096]{1,0:T(8,128)(2,1)} %all-gather.22.cloned.1.call-done) | non-fusion elementwise | flops 4194304 | bytes 25165824 | tf_op jit(solution)/shard_map/convert_element_type | solution.py:277
  999.5 54.4 %all-gather.24.cloned.1.call-done = bf16[4096,1024]{1,0:T(8,128)(2,1)} async-done(((bf16[256,1024]{1,0:T(8,128)(2,1)}), bf16[4096,1024]{1,0:T(8,128)(2,1)}) %all-gather.24.cloned.1.call-update) | async-done | bytes 8388624 | tf_op jit(solution)/shard_map/all_gather | solution.py:283
  1053.9 11.7 %convert_element_type.207 = f32[4096,1024]{1,0:T(8,128)} convert(bf16[4096,1024]{1,0:T(8,128)(2,1)} %all-gather.24.cloned.1.call-done) | non-fusion elementwise | flops 4194304 | bytes 25165824 | tf_op jit(solution)/shard_map/convert_element_type | solution.py:283
  (237 shorter events, 73.1 us)
Async XLA Ops:
  7.2 4.3 copy-start.5
  7.2 66.0 %copy-start.35 = (f32[1024]{0:T(1024)S(1)}, f32[1024]{0:T(1024)}, u32[]{:S(2)}) copy-start(f32[1024]{0:T(1024)} %param.20) | copy-start | bytes 12292
  7.2 66.0 %copy-start.28 = (f32[1024]{0:T(1024)S(1)}, f32[1024]{0:T(1024)}, u32[]{:S(2)}) copy-start(f32[1024]{0:T(1024)} %param.19) | copy-start | bytes 12292
  7.2 66.0 %all-gather.10.cloned.1.call-start = ((), (), s32[]{:S(2)}) async-start(), calls=%async_computation.8 | async-start | bytes 6684672 | tf_op jit(solution)/shard_map/all_gather | solution.py:152
  7.9 167.9 %all-gather.12.cloned.1.call-start = ((), (), s32[]{:S(2)}) async-start(), calls=%async_computation.9 | async-start | bytes 2228224 | tf_op jit(solution)/shard_map/all_gather | solution.py:153
  8.7 182.3 %all-gather.14.cloned.1.call-start = ((), (), s32[]{:S(2)}) async-start(), calls=%async_computation.10 | async-start | bytes 8912896 | tf_op jit(solution)/shard_map/all_gather | solution.py:154
  9.4 256.7 %all-gather.16.cloned.1.call-start = ((), (), s32[]{:S(2)}) async-start(), calls=%async_computation.11 | async-start | bytes 8912896 | tf_op jit(solution)/shard_map/all_gather | solution.py:155
  11.5 68.5 %copy-start.22 = (f32[512]{0:T(512)}, f32[512]{0:T(512)S(1)}, u32[]{:S(2)}) copy-start(f32[512]{0:T(512)S(1)} %broadcast_multiply_fusion.5) | copy-start | bytes 6148
  11.9 68.0 %copy-start.24 = (f32[512]{0:T(512)}, f32[512]{0:T(512)S(1)}, u32[]{:S(2)}) copy-start(f32[512]{0:T(512)S(1)} %add_rsqrt_fusion.1) | copy-start | bytes 6148
  83.2 5.4 copy-start.40
  83.2 41.4 %all-to-all-start = ((bf16[512,3,8,128]{3,0,1,2:T(8,128)(2,1)}), bf16[512,3,8,128]{3,0,1,2:T(8,128)(2,1)}, u32[]{:S(2)}, u32[]{:S(2)}) async-start(bf16[512,3,8,128]{3,0,1,2:T(8,128)(2,1)} %copy.87), calls=%async_computation | async-start | bytes 6291456 | tf_op jit(solution)/shard_map/all_to_all | solution.py:171
  175.9 15.1 %copy-start.27 = (f32[1024]{0:T(1024)S(1)}, f32[1024]{0:T(1024)}, u32[]{:S(2)}) copy-start(f32[1024]{0:T(1024)} %param.23) | copy-start | bytes 12292
  175.9 15.1 %copy-start.37 = (f32[1024]{0:T(1024)S(1)}, f32[1024]{0:T(1024)}, u32[]{:S(2)}) copy-start(f32[1024]{0:T(1024)} %param.24) | copy-start | bytes 12292
  179.5 109.6 %copy-start.3 = (f32[512,1024]{1,0:T(8,128)}, f32[512,1024]{1,0:T(8,128)S(1)}, u32[]{:S(2)}) copy-start(f32[512,1024]{1,0:T(8,128)S(1)} %get-tuple-element.282) | copy-start | bytes 6291460
  179.9 86.3 %copy-start.34 = (f32[4096]{0:T(1024)S(1)}, f32[4096]{0:T(1024)}, u32[]{:S(2)}) copy-start(f32[4096]{0:T(1024)} %param.26) | copy-start | bytes 49156
  266.1 15.3 %copy-start.33 = (bf16[1024,4096]{1,0:T(8,128)(2,1)S(1)}, bf16[1024,4096]{1,0:T(8,128)(2,1)}, u32[]{:S(2)}) copy-start(bf16[1024,4096]{1,0:T(8,128)(2,1)} %all-gather.14.cloned.1.call-done) | copy-start | bytes 25165828
  281.5 7.7 copy-start.13
  293.2 18.0 %all-to-all-start.2 = ((bf16[512,8,128]{2,0,1:T(8,128)(2,1)}), bf16[512,8,128]{2,0,1:T(8,128)(2,1)}, u32[]{:S(2)}, u32[]{:S(2)}) async-start(bf16[512,8,128]{2,0,1:T(8,128)(2,1)} %bitcast.93), calls=%async_computation.2 | async-start | bytes 2097152 | tf_op jit(solution)/shard_map/all_to_all | solution.py:203
  297.7 165.6 %reduce-scatter.7.cloned.1.call-start = ((), (), s32[]{:S(2)}) async-start(), calls=%async_computation.14 | async-start | bytes 2228224 | tf_op jit(solution)/shard_map/reduce_scatter | solution.py:224
  302.2 219.5 %reduce-scatter.5.cloned.1.call-start = ((), (), s32[]{:S(2)}) async-start(), calls=%async_computation.12 | async-start | bytes 6684672 | tf_op jit(solution)/shard_map/reduce_scatter | solution.py:221
  334.4 3.8 copy-start.8
  334.4 3.8 copy-start.15
  334.4 4.1 copy-start.18
  338.4 6.1 copy-start
  338.4 6.1 copy-start.20
  365.3 3.8 copy-start.15
  365.3 4.1 copy-start.18
  369.4 6.1 copy-start
  369.4 6.1 copy-start.20
  425.5 4.8 copy-start.6
  425.5 4.8 copy-start.23
  425.5 4.8 copy-start.25
  425.5 4.8 copy-start.29
  425.5 4.8 copy-start.36
  438.2 193.2 %reduce-scatter.9.cloned.1.call-start = ((), (), s32[]{:S(2)}) async-start(), calls=%async_computation.16 | async-start | bytes 8912896 | tf_op jit(solution)/shard_map/reduce_scatter | solution.py:233
  449.0 291.5 %reduce-scatter.11.cloned.1.call-start = ((), (), s32[]{:S(2)}) async-start(), calls=%async_computation.18 | async-start | bytes 8912896 | tf_op jit(solution)/shard_map/reduce_scatter | solution.py:239
  463.1 335.4 %copy-start.32 = (u32[32]{0:T(128)S(1)}, u32[32]{0:T(128)}, u32[]{:S(2)}) copy-start(u32[32]{0:T(128)} %constant.93) | copy-start | bytes 388
  463.1 337.9 %copy-start.39 = (f32[1024]{0:T(1024)S(1)}, f32[1024]{0:T(1024)}, u32[]{:S(2)}) copy-start(f32[1024]{0:T(1024)} %param.28) | copy-start | bytes 12292
  463.1 331.9 %all-reduce.17.cloned.1.call-start = ((), (), s32[]{:S(2)}) async-start(), calls=%async_computation.20 | async-start | bytes 3145728 | tf_op jit(solution)/shard_map/psum | solution.py:249
  740.5 233.5 %all-gather.20.cloned.1.call-start = ((), (), s32[]{:S(2)}) async-start(), calls=%async_computation.15 | async-start | bytes 2228224 | tf_op jit(solution)/shard_map/all_gather | solution.py:268
  795.0 183.1 %all-gather.18.cloned.1.call-start = ((), (), s32[]{:S(2)}) async-start(), calls=%async_computation.13 | async-start | bytes 6684672 | tf_op jit(solution)/shard_map/all_gather | solution.py:265
  795.8 191.6 %all-gather.22.cloned.1.call-start = ((), (), s32[]{:S(2)}) async-start(), calls=%async_computation.17 | async-start | bytes 8912896 | tf_op jit(solution)/shard_map/all_gather | solution.py:277
  796.3 257.6 %all-gather.24.cloned.1.call-start = ((), (), s32[]{:S(2)}) async-start(), calls=%async_computation.19 | async-start | bytes 8912896 | tf_op jit(solution)/shard_map/all_gather | solution.py:283
  801.1 12.5 %copy-start.14 = (bf16[512,3,2,4,128]{0,4,3,2,1:T(8,128)(2,1)S(1)}, bf16[512,3,2,4,128]{0,4,3,2,1:T(8,128)(2,1)}, u32[]{:S(2)}) copy-start(bf16[512,3,2,4,128]{0,4,3,2,1:T(8,128)(2,1)} %copy.100) | copy-start | bytes 9437188
  813.6 8.4 copy-start.30
  813.6 8.4 copy-start.31
  813.6 61.2 %copy-start.26 = (bf16[4096]{0:T(1024)(128)(2,1)S(1)}, bf16[4096]{0:T(1024)(128)(2,1)}, u32[]{:S(2)}) copy-start(bf16[4096]{0:T(1024)(128)(2,1)} %get-tuple-element.272) | copy-start | bytes 24580
  813.6 157.1 %copy-start.10 = (f32[512,1024]{1,0:T(8,128)S(1)}, f32[512,1024]{1,0:T(8,128)}, u32[]{:S(2)}) copy-start(f32[512,1024]{1,0:T(8,128)} %copy-done.9) | copy-start | bytes 6291460
  (21 other events, 40.8 us)
Sparse Core Ops, SparseCore 0:
  10.3 62.8 all-gather.9
  75.4 38.7 all-gather.11
  116.3 74.6 all-gather.13
  193.0 73.0 all-gather.15
  302.4 57.8 reduce-scatter.6
  438.3 83.4 reduce-scatter.4
  526.4 104.9 reduce-scatter.8
  636.0 104.4 reduce-scatter.10
  743.0 51.9 all-reduce.16
  797.2 40.2 all-gather.19
  840.1 62.2 all-gather.17
  904.6 73.8 all-gather.21
  980.8 73.0 all-gather.23
where the time goes:
time: 1080 us; the launch traced here: 1070 us
  waiting for transfers between devices  572 us (53%)
  blocking collectives  197 us (18%)
  matrix products  166 us (15%)
  other arithmetic  62.1 us (6%)
  local copies, waits for them, and re-layouts  40 us (4%)
  between operations  16.5 us (2%)
    reduce_scatter x1, waiting for transfers between devices, on_device(): lax.psum_scatter(grad_w_up.astype(jnp.bfloat16), 'dp', scatter_dimension=...  110 us
    reduce_scatter x1, waiting for transfers between devices, on_device(): lax.psum_scatter(grad_w_down.astype(jnp.bfloat16), 'dp', scatter_dimensio...  109 us
    unnamed x2, blocking collectives  107 us
    all_gather x1, waiting for transfers between devices, on_device(): lax.all_gather(w_down, 'dp', axis=0, tiled=True)  64.8 us
    all_gather x1, waiting for transfers between devices, on_device(): lax.all_gather(w_qkv, 'dp', axis=0, tiled=True)  61.3 us
    reduce_scatter x1, waiting for transfers between devices, on_device(): lax.psum_scatter(grad_w_qkv.astype(jnp.bfloat16), 'dp', scatter_dimension...  58.5 us
    all_gather x1, waiting for transfers between devices, on_device(): lax.all_gather(all_part[8].astype(jnp.bfloat16), 'dp', axis=0, tiled=True)  54.4 us
    psum x1, waiting for transfers between devices, on_device(): lax.psum(all_part[2].astype(jnp.bfloat16), 'seq').astype(jnp.float32)  54.4 us
  transfers between devices with their start and end apart: 15, of which 10 were waited for; matrix products, arithmetic and copies ran while one was open for 21% of the time, Pallas kernels for 0%

commit v1 on v0

--- a/solution.py
+++ b/solution.py
@@ -1,6 +1,10 @@
+import functools
+
 import jax
 import jax.numpy as jnp
 from jax import lax
+from jax.experimental import pallas as pl
+from jax.experimental.pallas import tpu as pltpu
 from jax.sharding import PartitionSpec as P
 
 HEADS = 8
@@ -303,9 +307,741 @@
     )
 
 
+MESH = pl.DeviceIdType.MESH
+
+
+class Place:
+    def __init__(self, n_z):
+        dp = lax.axis_index("dp")
+        self.n_z = n_z
+        self.dp = dp
+        self.y = lax.axis_index("seq")
+        self.core = dp % 2
+        self.chip = dp // 2
+        self.x = self.chip % 2
+        self.z = self.chip // 2
+        self.quarter = 2 * self.core + self.y
+
+    def device(self, z=None, x=None, core=None, y=None):
+        z = self.z if z is None else z
+        x = self.x if x is None else x
+        core = self.core if core is None else core
+        y = self.y if y is None else y
+        return ((z * 2 + x) * 2 + core, y)
+
+    def across_core(self):
+        return self.device(core=1 - self.core)
+
+    def across_x(self):
+        return self.device(x=1 - self.x)
+
+    def across_y(self):
+        return self.device(y=1 - self.y)
+
+    def z_after(self, k):
+        return (self.z + k) % self.n_z
+
+    def z_before(self, k):
+        return (self.z + self.n_z - k) % self.n_z
+
+    def along_z(self, k):
+        return self.device(z=self.z_after(k))
+
+
+class Copies:
+    def __init__(self, send, recv, near):
+        self.send, self.recv, self.near = send, recv, near
+        self.sent, self.held, self.n, self.m = [], [], 0, 0
+
+    def remote(self, src, dst, device):
+        copy = pltpu.make_async_remote_copy(
+            src_ref=src,
+            dst_ref=dst,
+            send_sem=self.send.at[self.n],
+            recv_sem=self.recv.at[self.n],
+            device_id=device,
+            device_id_type=MESH,
+        )
+        self.n += 1
+        copy.start()
+        self.sent.append(copy)
+        self.held.append(copy)
+        return copy
+
+    def local(self, src, dst):
+        copy = pltpu.make_async_copy(src, dst, self.near.at[self.m])
+        self.m += 1
+        copy.start()
+        return copy
+
+    def arrive(self, *copies):
+        for copy in copies:
+            copy.wait_recv()
+            self.held = [other for other in self.held if other is not copy]
+
+    def finish(self):
+        for copy in self.held:
+            copy.wait_recv()
+        for copy in self.sent:
+            copy.wait_send()
+        self.held, self.sent = [], []
+
+
+def meet(devices):
+    barrier = pltpu.get_barrier_semaphore()
+    for device in devices:
+        pl.semaphore_signal(barrier, inc=1, device_id=device, device_id_type=MESH)
+    pl.semaphore_wait(barrier, len(devices))
+
+
+def at(start, size, unit):
+    return pl.ds(pl.multiple_of(start, unit), size)
+
+
+def communicate(kernel, out_shapes, ins, out_specs, in_specs, counts, scratch=(), call_id=0, limit=None):
+    return pl.pallas_call(
+        kernel,
+        out_shape=out_shapes,
+        in_specs=in_specs,
+        out_specs=out_specs,
+        scratch_shapes=list(scratch)
+        + [
+            pltpu.SemaphoreType.DMA((counts[0],)),
+            pltpu.SemaphoreType.DMA((counts[0],)),
+            pltpu.SemaphoreType.DMA((counts[1],)),
+        ],
+        compiler_params=pltpu.CompilerParams(
+            collective_id=call_id, has_side_effects=True, vmem_limit_bytes=limit or (56 << 20)
+        ),
+    )(*ins)
+
+
+HBM = pl.BlockSpec(memory_space=pltpu.HBM)
+VMEM = pl.BlockSpec(memory_space=pltpu.VMEM)
+SMEM = pl.BlockSpec(memory_space=pltpu.SMEM)
+
+
+def gather_kernel(n_z, wq, wo, wu, wd, tok, cot, lens, WQ, WO, WU, WD, XQ, CQ, LQ, send, recv, near):
+    me = Place(n_z)
+    run = Copies(send, recv, near)
+    quarter, other = me.quarter, 2 * (1 - me.core) + me.y
+    rows = wq.shape[0]
+    third = wq.shape[1] // 3
+    cut = third // 4
+    chips = 2 * n_z
+    span = wu.shape[1] // chips
+    unit = span // 4
+    meet(
+        [me.across_core(), me.across_x(), me.across_y()] + [me.along_z(k) for k in range(1, n_z)]
+    )
+    mine = at(me.dp * rows, rows, 16)
+    pair = at(me.chip * 2 * rows, 2 * rows, 16)
+
+    def pair_of(z):
+        return at((z * 2 + me.x) * 2 * rows, 2 * rows, 16)
+
+    begun = []
+    landed_q = []
+    for p in range(3):
+        into = WQ.at[mine, p * cut : (p + 1) * cut]
+        begun.append(run.local(wq.at[:, at(p * third + quarter * cut, cut, 128)], into))
+        landed_q.append(
+            run.remote(wq.at[:, at(p * third + other * cut, cut, 128)], into, me.across_core())
+        )
+    block = tok.shape[0]
+    half = block // 2
+
+    def spread(src, dst):
+        keep = run.local(src, dst.at[quarter])
+        over = [
+            run.remote(src.at[h * half : (h + 1) * half], dst.at[quarter, h * half : (h + 1) * half], me.across_y())
+            for h in range(2)
+        ]
+        run.remote(src, dst.at[quarter], me.across_core())
+        return keep, over
+
+    def pass_on(over, dst):
+        slot = 2 * me.core + 1 - me.y
+        for h in range(2):
+            run.arrive(over[h])
+            part = dst.at[slot, h * half : (h + 1) * half]
+            run.remote(part, part, me.across_core())
+
+    last = [run.local(lens, LQ.at[me.core])]
+    run.remote(lens, LQ.at[me.core], me.across_core())
+    keep_x, over_x = spread(tok, XQ)
+    last.append(keep_x)
+    landed_u, begun_u = [], []
+    for s in range(chips):
+        into = WU.at[mine, s * unit : (s + 1) * unit]
+        begun_u.append(run.local(wu.at[:, at(s * span + quarter * unit, unit, 128)], into))
+        landed_u.append(
+            run.remote(wu.at[:, at(s * span + other * unit, unit, 128)], into, me.across_core())
+        )
+    for copy in begun:
+        copy.wait()
+    run.arrive(*landed_q)
+    part = WQ.at[pair]
+    from_z = {"q": [run.remote(part, part, me.along_z(k)) for k in range(1, n_z)]}
+    run.remote(part, part, me.across_x())
+    from_z["o"] = [run.remote(wo, WO.at[mine], me.along_z(k)) for k in range(1, n_z)]
+    from_x = [run.remote(wo, WO.at[mine], me.across_x())]
+    run.remote(wo, WO.at[mine], me.across_core())
+    last.append(run.local(wo, WO.at[mine]))
+    for copy in begun_u:
+        copy.wait()
+    run.arrive(*landed_u)
+    part = WU.at[pair]
+    from_z["u"] = [run.remote(part, part, me.along_z(k)) for k in range(1, n_z)]
+    run.remote(part, part, me.across_x())
+    own = wd.at[at(me.y * unit, unit, 16)]
+    into = WD.at[at(me.chip * unit, unit, 16)]
+    from_z["d"] = [run.remote(own, into, me.along_z(k)) for k in range(1, n_z)]
+    run.remote(own, into, me.across_x())
+    last.append(run.local(own, into))
+    keep_c, over_c = spread(cot, CQ)
+    last.append(keep_c)
+
+    for k in range(1, n_z):
+        z = me.z_before(k)
+        run.arrive(from_z["q"][k - 1])
+        part = WQ.at[pair_of(z)]
+        run.remote(part, part, me.across_x())
+    pass_on(over_x, XQ)
+    for k in range(1, n_z):
+        z = me.z_before(k)
+        run.arrive(from_z["o"][k - 1])
+        part = WO.at[at(((z * 2 + me.x) * 2 + me.core) * rows, rows, 16)]
+        from_x.append(run.remote(part, part, me.across_x()))
+        run.remote(part, part, me.across_core())
+    for k in range(1, n_z):
+        z = me.z_before(k)
+        run.arrive(from_z["u"][k - 1])
+        part = WU.at[pair_of(z)]
+        run.remote(part, part, me.across_x())
+    for k in range(1, n_z):
+        z = me.z_before(k)
+        run.arrive(from_z["d"][k - 1])
+        part = WD.at[at((z * 2 + me.x) * unit, unit, 16)]
+        run.remote(part, part, me.across_x())
+    pass_on(over_c, CQ)
+    for k in range(n_z):
+        z = me.z_before(k)
+        run.arrive(from_x[k])
+        part = WO.at[at(((z * 2 + 1 - me.x) * 2 + me.core) * rows, rows, 16)]
+        run.remote(part, part, me.across_core())
+    run.finish()
+    for copy in last:
+        copy.wait()
+
+
+def gather_all(n_z, wq, wo, wu, wd, tok, cot, lens):
+    width, low = wq.shape[0] * 4 * n_z, jnp.bfloat16
+    quarter_ff = wu.shape[1] // 4
+    shapes = [
+        jax.ShapeDtypeStruct((width, wq.shape[1] // 4), low),
+        jax.ShapeDtypeStruct((width, width), low),
+        jax.ShapeDtypeStruct((width, quarter_ff), low),
+        jax.ShapeDtypeStruct((quarter_ff, width), low),
+        jax.ShapeDtypeStruct((4,) + tok.shape, low),
+        jax.ShapeDtypeStruct((4,) + tok.shape, low),
+        jax.ShapeDtypeStruct((2,) + lens.shape, lens.dtype),
+    ]
+    return communicate(
+        functools.partial(gather_kernel, n_z),
+        shapes,
+        (wq, wo, wu, wd, tok, cot, lens),
+        [HBM] * 7,
+        [HBM] * 7,
+        (96, 24),
+        call_id=1,
+    )
+
+
+def quad_columns_kernel(n_z, src, dst, send, recv, near):
+    me = Place(n_z)
+    run = Copies(send, recv, near)
+    rows, cols = src.shape
+    parts = 4
+    step = rows // parts
+    meet([me.across_core(), me.across_y()])
+
+    def place(quarter, i):
+        return dst.at[i * step : (i + 1) * step, at(quarter * cols, cols, 128)]
+
+    over = []
+    for i in range(parts):
+        over.append(
+            run.remote(src.at[i * step : (i + 1) * step], place(me.quarter, i), me.across_y())
+        )
+    keep = run.local(src, dst.at[:, at(me.quarter * cols, cols, 128)])
+    run.remote(src, dst.at[:, at(me.quarter * cols, cols, 128)], me.across_core())
+    for i in range(parts):
+        run.arrive(over[i])
+        part = place(2 * me.core + 1 - me.y, i)
+        run.remote(part, part, me.across_core())
+    run.finish()
+    keep.wait()
+
+
+def quad_columns(n_z, src):
+    return communicate(
+        functools.partial(quad_columns_kernel, n_z),
+        jax.ShapeDtypeStruct((src.shape[0], 4 * src.shape[1]), src.dtype),
+        (src,),
+        HBM,
+        [HBM],
+        (12, 1),
+        call_id=2,
+    )
+
+
+def quad_blocks_kernel(n_z, src, dst, send, recv, near):
+    me = Place(n_z)
+    run = Copies(send, recv, near)
+    rows = src.shape[0]
+    parts = 4
+    step = rows // parts
+    meet([me.across_core(), me.across_y()])
+    over = []
+    for i in range(parts):
+        cut = slice(i * step, (i + 1) * step)
+        over.append(run.remote(src.at[cut], dst.at[me.quarter, cut], me.across_y()))
+    keep = run.local(src, dst.at[me.quarter])
+    run.remote(src, dst.at[me.quarter], me.across_core())
+    for i in range(parts):
+        run.arrive(over[i])
+        part = dst.at[2 * me.core + 1 - me.y, i * step : (i + 1) * step]
+        run.remote(part, part, me.across_core())
+    run.finish()
+    keep.wait()
+
+
+def quad_blocks(n_z, src):
+    return communicate(
+        functools.partial(quad_blocks_kernel, n_z),
+        jax.ShapeDtypeStruct((4,) + src.shape, src.dtype),
+        (src,),
+        HBM,
+        [HBM],
+        (12, 1),
+        call_id=3,
+    )
+
+
+def add(*values):
+    total = values[0].astype(jnp.float32)
+    for value in values[1:]:
+        total = total + value.astype(jnp.float32)
+    return total
+
+
+def reduce_kernel(n_z, n_quad, n_chip, *refs):
+    me = Place(n_z)
+    n_in = n_quad + n_chip
+    ins, outs, rest = refs[:n_in], refs[n_in : 2 * n_in], refs[2 * n_in :]
+    scratch, (send, recv, near) = rest[:-3], rest[-3:]
+    run = Copies(send, recv, near)
+    devices = [me.across_core(), me.across_y()]
+    if n_chip:
+        devices += [me.across_x()] + [me.along_z(k) for k in range(1, n_z)]
+    meet(devices)
+    quad_scratch = [scratch[3 * i : 3 * i + 3] for i in range(n_quad)]
+    chip_scratch = [scratch[3 * n_quad + 3 * i : 3 * n_quad + 3 * i + 3] for i in range(n_chip)]
+    order = [1 - me.y, me.y]
+
+    def quad_start(i):
+        near_recv = quad_scratch[i][0]
+        return [
+            run.remote(ins[i].at[2 * (1 - me.core) + y], near_recv.at[y], me.across_core()) for y in order
+        ]
+
+    def chip_start(i):
+        far_recv = chip_scratch[i][0]
+        sent = []
+        for k in range(1, n_z + 1):
+            z = me.z_after(k)
+            sent.append(
+                run.remote(ins[n_quad + i].at[z * 2 + 1 - me.x], far_recv.at[z], me.across_x())
+            )
+        return sent
+
+    near_sent = [quad_start(i) for i in range(n_quad)]
+    x_sent = [chip_start(i) for i in range(n_chip)]
+    y_sent = []
+    for i in range(n_quad):
+        near_recv, over_send, over_recv = quad_scratch[i]
+        run.arrive(near_sent[i][0])
+        over_send[...] = add(ins[i][2 * me.core + 1 - me.y], near_recv[1 - me.y]).astype(jnp.bfloat16)
+        y_sent.append(run.remote(over_send, over_recv, me.across_y()))
+    z_sent = []
+    for k in range(1, n_z + 1):
+        z = me.z_after(k)
+        for i in range(n_chip):
+            far_recv, z_send, z_recv = chip_scratch[i]
+            run.arrive(x_sent[i][k - 1])
+            z_send[z] = add(ins[n_quad + i][z * 2 + me.x], far_recv[z]).astype(jnp.bfloat16)
+            if k < n_z:
+                z_sent.append(run.remote(z_send.at[z], z_recv.at[k - 1], me.along_z(k)))
+    for i in range(n_quad):
+        near_recv, over_send, over_recv = quad_scratch[i]
+        run.arrive(near_sent[i][1], y_sent[i])
+        outs[i][...] = add(ins[i][2 * me.core + me.y], near_recv[me.y], over_recv[...])
+    run.arrive(*z_sent)
+    for i in range(n_chip):
+        far_recv, z_send, z_recv = chip_scratch[i]
+        outs[n_quad + i][...] = add(z_send[me.z], *[z_recv[k] for k in range(n_z - 1)]).astype(
+            jnp.bfloat16
+        )
+    run.finish()
+
+
+def reduce_all(n_z, quads, chips, call_id):
+    scratch, shapes = [], []
+    for value in quads:
+        block = value.shape[1:]
+        scratch += [
+            pltpu.VMEM((2,) + block, jnp.bfloat16),
+            pltpu.VMEM(block, jnp.bfloat16),
+            pltpu.VMEM(block, jnp.bfloat16),
+        ]
+        shapes.append(jax.ShapeDtypeStruct(block, jnp.float32))
+    for value in chips:
+        block = value.shape[1:]
+        scratch += [
+            pltpu.VMEM((n_z,) + block, jnp.bfloat16),
+            pltpu.VMEM((n_z,) + block, jnp.bfloat16),
+            pltpu.VMEM((n_z - 1,) + block, jnp.bfloat16),
+        ]
+        shapes.append(jax.ShapeDtypeStruct(block, jnp.bfloat16))
+    n = len(quads) + len(chips)
+    return communicate(
+        functools.partial(reduce_kernel, n_z, len(quads), len(chips)),
+        shapes,
+        tuple(quads) + tuple(chips),
+        [VMEM] * n,
+        [VMEM] * n,
+        (3 * len(quads) + (2 * n_z - 1) * len(chips) + 1, 1),
+        scratch,
+        call_id=call_id,
+    )
+
+
+def share_kernel(n_z, n_parts, src, dst, send, recv, near):
+    me = Place(n_z)
+    run = Copies(send, recv, near)
+    step = src.shape[0] // n_parts
+    half = step // 2
+    meet(
+        [me.across_core(), me.across_x(), me.across_y()] + [me.along_z(k) for k in range(1, n_z)]
+    )
+
+    def slot(z, x, y):
+        return ((z * 2 + x) * 2 + me.core) * 2 + y
+
+    own = slot(me.z, me.x, me.y)
+    keep = run.local(src, dst.at[own])
+    run.remote(src, dst.at[own], me.across_core())
+    spans = [
+        (slice(p * step, p * step + half), slice(p * step + half, (p + 1) * step), slice(p * step, (p + 1) * step))
+        for p in range(n_parts)
+    ]
+    from_z = {}
+    for p, (_, _, whole) in enumerate(spans):
+        for k in range(1, n_z):
+            from_z[k, p] = run.remote(src.at[whole], dst.at[own, whole], me.along_z(k))
+    level = {}
+
+    def fan(k, p):
+        first, second, whole = spans[p]
+        here = dst.at[slot(me.z_before(k), me.x, me.y)]
+        there = here if k else src
+        level["xa", k, p] = run.remote(there.at[first], here.at[first], me.across_x())
+        level["yb", k, p] = run.remote(there.at[second], here.at[second], me.across_y())
+        level["ya", k, p] = run.remote(there.at[first], here.at[first], me.across_y())
+        level["xb", k, p] = run.remote(there.at[second], here.at[second], me.across_x())
+        if k:
+            run.remote(here.at[whole], here.at[whole], me.across_core())
+
+    def relay(k, p):
+        first, second, _ = spans[p]
+        z = me.z_before(k)
+        run.arrive(level["xa", k, p])
+        part = dst.at[slot(z, 1 - me.x, me.y), first]
+        level["late a", k, p] = run.remote(part, part, me.across_y())
+        run.arrive(level["yb", k, p])
+        part = dst.at[slot(z, me.x, 1 - me.y), second]
+        level["late b", k, p] = run.remote(part, part, me.across_x())
+
+    def hand_over(k, p):
+        whole = spans[p][2]
+        z = me.z_before(k)
+        run.arrive(level["xb", k, p])
+        part = dst.at[slot(z, 1 - me.x, me.y), whole]
+        run.remote(part, part, me.across_core())
+        run.arrive(level["ya", k, p])
+        part = dst.at[slot(z, me.x, 1 - me.y), whole]
+        run.remote(part, part, me.across_core())
+
+    def hand_last(k, p):
+        run.arrive(level["late a", k, p], level["late b", k, p])
+        part = dst.at[slot(me.z_before(k), 1 - me.x, 1 - me.y), spans[p][2]]
+        run.remote(part, part, me.across_core())
+
+    steps = [(k, p) for k in range(n_z) for p in range(n_parts)]
+    for i in range(len(steps) + 3):
+        if i < len(steps):
+            k, p = steps[i]
+            if k:
+                run.arrive(from_z[k, p])
+            fan(k, p)
+        if 1 <= i < len(steps) + 1:
+            relay(*steps[i - 1])
+        if 2 <= i < len(steps) + 2:
+            hand_over(*steps[i - 2])
+        if 3 <= i < len(steps) + 3:
+            hand_last(*steps[i - 3])
+    run.finish()
+    keep.wait()
+
+
+def share_all(n_z, src, n_parts, call_id):
+    return communicate(
+        functools.partial(share_kernel, n_z, n_parts),
+        jax.ShapeDtypeStruct((8 * n_z,) + src.shape, src.dtype),
+        (src,),
+        HBM,
+        [HBM],
+        (n_parts * (n_z * 10 + n_z) + 1, 1),
+        call_id=call_id,
+    )
+
+
+def allowed_and_bias(first, rows, count, ends, slope):
+    row = first + lax.broadcasted_iota(jnp.int32, (rows, 1), 0)
+    col = lax.broadcasted_iota(jnp.int32, (1, count), 1)
+    begin = jnp.zeros((rows, 1), jnp.int32)
+    for end in ends:
+        begin = jnp.where(row >= end, end, begin)
+    allowed = (col >= begin) & (col <= row)
+    bias = slope * (col - first).astype(jnp.float32)
+    return allowed, bias
+
+
+NEVER = -1000000000.0
+
+
+def attend_kernel(slopes, ends, q, k, v, o, lse):
+    group, head = pl.program_id(0), pl.program_id(1)
+    count, size = q.shape
+    rows = min(256, count)
+    slope = slopes[head]
+    stops = [ends[group, i] for i in range(ends.shape[1] - 1)]
+    for first in range(0, count, rows):
+        here = slice(first, first + rows)
+        seen = first + rows
+        allowed, bias = allowed_and_bias(first, rows, seen, stops, slope)
+        s = times_transposed(q[here], k[:seen]) * size**-0.5 + bias
+        s = jnp.where(allowed, s, NEVER)
+        top = jnp.max(s, axis=-1, keepdims=True)
+        w = jnp.exp(s - top)
+        total = jnp.sum(w, axis=-1, keepdims=True)
+        p = (w * (1.0 / total)).astype(jnp.bfloat16)
+        o[here] = jnp.dot(p, v[:seen], preferred_element_type=jnp.float32).astype(jnp.bfloat16)
+        lse[here] = top + jnp.log(total)
+
+
+def attend_back_kernel(slopes, ends, q, k, v, o, lse, do, dq, dk, dv, sum_k, sum_v):
+    group, head = pl.program_id(0), pl.program_id(1)
+    count, size = q.shape
+    rows = min(256, count)
+    slope = slopes[head]
+    scale = size**-0.5
+    stops = [ends[group, i] for i in range(ends.shape[1] - 1)]
+    sum_k[...] = jnp.zeros_like(sum_k)
+    sum_v[...] = jnp.zeros_like(sum_v)
+    for first in range(0, count, rows):
+        here = slice(first, first + rows)
+        seen = first + rows
+        allowed, bias = allowed_and_bias(first, rows, seen, stops, slope)
+        s = times_transposed(q[here], k[:seen]) * scale + bias
+        p = jnp.exp(jnp.where(allowed, s, NEVER) - lse[here])
+        grad = do[here]
+        dots = jnp.sum(grad.astype(jnp.float32) * o[here].astype(jnp.float32), axis=-1, keepdims=True)
+        sum_v[:seen] += inner_rows(p.astype(jnp.bfloat16), grad)
+        ds = (p * (times_transposed(grad, v[:seen]) - dots)).astype(jnp.bfloat16)
+        dq[here] = (jnp.dot(ds, k[:seen], preferred_element_type=jnp.float32) * scale).astype(jnp.bfloat16)
+        sum_k[:seen] += inner_rows(ds, q[here])
+    dk[...] = (sum_k[...] * scale).astype(jnp.bfloat16)
+    dv[...] = sum_v[...].astype(jnp.bfloat16)
+
+
+def head_spec(count, size, offset):
+    return pl.BlockSpec((count, size), lambda g, h: (g, offset + h))
+
+
+def attention(qkv, slopes, ends, count, size):
+    groups, heads = qkv.shape[0] // count, qkv.shape[1] // size // 3
+    return pl.pallas_call(
+        attend_kernel,
+        grid=(groups, heads),
+        in_specs=[SMEM, SMEM] + [head_spec(count, size, heads * i) for i in range(3)],
+        out_specs=[head_spec(count, size, 0), pl.BlockSpec((None, None, count, 1), lambda g, h: (g, h, 0, 0))],
+        out_shape=[
+            jax.ShapeDtypeStruct((qkv.shape[0], heads * size), jnp.bfloat16),
+            jax.ShapeDtypeStruct((groups, heads, count, 1), jnp.float32),
+        ],
+        compiler_params=pltpu.CompilerParams(vmem_limit_bytes=48 << 20),
+    )(slopes, ends, qkv, qkv, qkv)
+
+
+def attention_back(qkv, o, lse, do, slopes, ends, count, size):
+    groups, heads = qkv.shape[0] // count, qkv.shape[1] // size // 3
+    own = head_spec(count, size, 0)
+    shape = jax.ShapeDtypeStruct((qkv.shape[0], heads * size), jnp.bfloat16)
+    return pl.pallas_call(
+        attend_back_kernel,
+        grid=(groups, heads),
+        in_specs=[SMEM, SMEM]
+        + [head_spec(count, size, heads * i) for i in range(3)]
+        + [own, pl.BlockSpec((None, None, count, 1), lambda g, h: (g, h, 0, 0)), own],
+        out_specs=[own] * 3,
+        out_shape=[shape] * 3,
+        scratch_shapes=[pltpu.VMEM((count, size), jnp.float32)] * 2,
+        compiler_params=pltpu.CompilerParams(vmem_limit_bytes=48 << 20),
+    )(slopes, ends, qkv, qkv, qkv, o, lse, do)
+
+
+def on_quad(
+    tokens,
+    lengths,
+    attn_gain,
+    attn_shift,
+    w_qkv,
+    w_out,
+    ffn_gain,
+    ffn_shift,
+    w_up,
+    b_up,
+    w_down,
+    b_down,
+    cotangent,
+):
+    low = jnp.bfloat16
+    local, width = tokens.shape
+    n_dp = lax.axis_size("dp")
+    n_z, chips = n_dp // 4, n_dp // 2
+    size = width // HEADS
+    heads = HEADS // 4
+    count = 2 * local
+    me = Place(n_z)
+    lens = jnp.zeros((8, 128), jnp.int32).at[:1, : lengths.shape[1]].set(lengths)
+    WQ, WO, WU, WD, XQ, CQ, LQ = gather_all(n_z, w_qkv, w_out, w_up, w_down, tokens, cotangent, lens)
+    ends = jnp.cumsum(LQ[:, 0, : lengths.shape[1]], axis=1, dtype=jnp.int32)
+    slopes = jnp.exp2(-(me.quarter * heads + jnp.arange(heads, dtype=jnp.int32) + 1).astype(jnp.float32))
+
+    h1 = norm_forward(XQ.reshape(4 * local, width).astype(jnp.float32), attn_gain, attn_shift)[0].astype(low)
+    qkv = jnp.dot(h1, WQ, preferred_element_type=jnp.float32).astype(low)
+    o, lse = attention(qkv, slopes, ends, count, size)
+    joined = quad_columns(n_z, o)
+    middle = XQ.reshape(4 * local, width).astype(jnp.float32) + jnp.dot(
+        joined, WO, preferred_element_type=jnp.float32
+    )
+    h2 = norm_forward(middle, ffn_gain, ffn_shift)[0].astype(low)
+    middle = lax.dynamic_slice_in_dim(middle, me.quarter * local, local)
+    _, unit_mid, factor_mid = norm_forward(middle, ffn_gain, ffn_shift)
+
+    unit = w_up.shape[1] // chips // 4
+    bias = lax.dynamic_index_in_dim(b_up.reshape(chips, 4, unit), me.quarter, 1, keepdims=False).reshape(-1)
+    c = CQ.reshape(4 * local, width)
+    pre = jnp.dot(h2, WU, preferred_element_type=jnp.float32) + bias
+    act, pull = jax.vjp(smooth_act, pre)
+    active = act.astype(low)
+    grad_pre = pull(times_transposed(c, WD))[0]
+    grad_pre_low = grad_pre.astype(low)
+    part_out = jnp.dot(active, WD, preferred_element_type=jnp.float32).astype(low)
+    part_h2 = times_transposed(grad_pre_low, WU).astype(low)
+    part_down = inner_rows(active, c).astype(low)
+    part_up = inner_rows(h2, grad_pre_low).astype(low)
+    grad_b_up = jnp.sum(grad_pre, axis=0)
+    sum_h2, sum_out, sum_down, sum_up = reduce_all(
+        n_z,
+        [part_h2.reshape(4, local, width), part_out.reshape(4, local, width)],
+        [part_down.reshape(chips, -1, width), part_up.reshape(chips, -1, part_up.shape[1])],
+        4,
+    )
+    block_out = (middle + sum_out + b_down).astype(low)
+    grad_out = cotangent.astype(jnp.float32)
+    grad_mid_norm, grad_ffn_gain, grad_ffn_shift = norm_backward(sum_h2, unit_mid, factor_mid, ffn_gain)
+    grad_middle = grad_out + grad_mid_norm
+    branch = quad_blocks(n_z, grad_middle.astype(low)).reshape(4 * local, width)
+    mine = lax.dynamic_slice_in_dim(WO, me.quarter * heads * size, heads * size)
+    part_w_out = inner_rows(o, branch).astype(low)
+    do = times_transposed(branch, mine).astype(low)
+    dqkv = jnp.concatenate(attention_back(qkv, o, lse, do, slopes, ends, count, size), axis=1)
+    part_qkv = inner_rows(h1, dqkv).astype(low)
+    part_h1 = times_transposed(dqkv, WQ).astype(low)
+    sum_h1, sum_qkv, sum_w_out = reduce_all(
+        n_z,
+        [part_h1.reshape(4, local, width)],
+        [part_qkv.reshape(chips, -1, part_qkv.shape[1]), part_w_out.reshape(chips, -1, width)],
+        5,
+    )
+    _, unit_in, factor_in = norm_forward(tokens.astype(jnp.float32), attn_gain, attn_shift)
+    grad_in_norm, grad_attn_gain, grad_attn_shift = norm_backward(sum_h1, unit_in, factor_in, attn_gain)
+    grad_tokens = (grad_middle + grad_in_norm).astype(low)
+
+    rows = sum_qkv.shape[0]
+    few = sum_w_out.shape[0]
+    across = rows // few
+    side = jnp.concatenate([sum_w_out[:, i * (width // across) : (i + 1) * (width // across)] for i in range(across)])
+    slab = jnp.concatenate([sum_down, sum_up, jnp.concatenate([sum_qkv, side], axis=1)])
+    shared = share_all(n_z, slab, 3, 6).reshape(chips, 4, 3, rows, width)
+    f32 = jnp.float32
+    grad_w_down = shared[:, :, 0].reshape(-1, width).astype(f32)
+    up = shared[:, :, 1].reshape(chips, 4, rows, chips, unit)
+    grad_w_up = jnp.transpose(up, (0, 2, 3, 1, 4)).reshape(width, -1).astype(f32)
+    three = shared[:, :, 2, :, : 3 * heads * size].reshape(chips, 4, rows, 3, heads * size)
+    grad_w_qkv = jnp.transpose(three, (0, 2, 3, 1, 4)).reshape(width, -1).astype(f32)
+    side = shared[:, :, 2, :, 3 * heads * size :].reshape(chips, 4, across, few, width // across)
+    grad_w_out = jnp.transpose(side, (1, 0, 3, 2, 4)).reshape(width, width).astype(f32)
+
+    spread = jnp.zeros((chips, 4, unit), f32)
+    spread = lax.dynamic_update_slice(spread, grad_b_up.reshape(chips, 1, unit), (0, me.quarter, 0))
+    small = jnp.concatenate(
+        [
+            spread.reshape(-1),
+            grad_attn_gain,
+            grad_attn_shift,
+            grad_ffn_gain,
+            grad_ffn_shift,
+            jnp.sum(grad_out, axis=0),
+        ]
+    )
+    small = lax.psum(small, ("dp", "seq"))
+    ff = w_up.shape[1]
+    vectors = [small[ff + i * width : ff + (i + 1) * width] for i in range(5)]
+    return (
+        block_out,
+        grad_tokens,
+        vectors[0],
+        vectors[1],
+        grad_w_qkv,
+        grad_w_out,
+        vectors[2],
+        vectors[3],
+        grad_w_up,
+        small[:ff],
+        grad_w_down,
+        vectors[4],
+    )
+
+
 def solution(mesh):
+    n_dp, n_seq = mesh.shape["dp"], mesh.shape["seq"]
+    quad = n_seq == 2 and n_dp % 4 == 0 and n_dp >= 8 and n_dp <= 16
     return jax.shard_map(
-        on_device,
+        on_quad if quad else on_device,
         mesh=mesh,
         in_specs=(
             P(("dp", "seq"), None),

time: 1080 us -> 743 us (0.69)
  waiting for transfers between devices: 572 us -> 0 us
  Pallas kernels: 0 us -> 458 us
  blocking collectives: 197 us -> 43.7 us
  matrix products: 166 us -> 70.1 us
  local copies, waits for them, and re-layouts: 40 us -> 101 us
  between operations: 16.5 us -> 1.69 us
    pallas_call x0 -> x8, Pallas kernels: none -> 458 us  [the longest x6 433 us: communicate(): pl.pallas_call(kernel, out_shape=out_shapes, in_specs=in_specs, out_specs...]
    reduce_scatter x4 -> x0, waiting for transfers between devices: 277 us -> none  [the longest x1 110 us: on_device(): lax.psum_scatter(grad_w_up.astype(jnp.bfloat16), 'dp', scatter_dimension=...]
    all_gather x8 -> x0, waiting for transfers between devices: 192 us -> none  [the longest x1 64.8 us: on_device(): lax.all_gather(w_down, 'dp', axis=0, tiled=True)]
    unnamed x2 -> x0, blocking collectives: 107 us -> none
    dot_general x18 -> x4, matrix products: 98.2 us -> 22.8 us  [the longest x1 6.98 us: on_quad(): jnp.dot(active, WD, preferred_element_type=jnp.float32).astype(low)]
    psum x1 -> x0, waiting for transfers between devices: 54.4 us -> none  [on_device(): lax.psum(all_part[2].astype(jnp.bfloat16), 'seq').astype(jnp.float32)]
    all_to_all x2 -> x0, blocking collectives: 53.5 us -> none  [the longest x1 37.9 us: on_device(): lax.all_to_all(grad_qkv_heads, 'seq', split_axis=0, concat_axis=2, tiled=...]
    unnamed x75 -> x72, local copies, waits for them, and re-layouts: 5.41 us -> 55 us
  transfers between devices with their start and end apart: 15 -> 0, of which waited for: 10 -> 0; matrix products, arithmetic and copies ran while one was open for 21% -> 0% of each run, Pallas kernels for 0% -> 0%
where the time goes in v1:
time: 743 us; the launch traced here: 733 us
  Pallas kernels  458 us (62%)
  local copies, waits for them, and re-layouts  101 us (14%)
  matrix products  70.1 us (9%)
  other arithmetic  58.4 us (8%)
  blocking collectives  43.7 us (6%)
    pallas_call x6, Pallas kernels, communicate(): pl.pallas_call(kernel, out_shape=out_shapes, in_specs=in_specs, out_specs...  433 us
    unnamed x72, local copies, waits for them, and re-layouts  55 us
    psum x1, blocking collectives, on_quad(): small = lax.psum(small, ('dp', 'seq'))  43.7 us
    convert_element_type x2, local copies, waits for them, and re-layouts, on_quad(): jnp.transpose(up, (0, 2, 3, 1, 4)).reshape(width, -1).astype(f32)  32.2 us
    dot_general x4, matrix products, times_transposed(): lax.dot_general(left, right, (((1,), (1,)), ((), ())), preferred_element_...  28.2 us
    dot_general x4, matrix products, inner_rows(): lax.dot_general(left, right, (((0,), (0,)), ((), ())), preferred_element_...  19.2 us

profile of v1, /device:TPU:17, one launch (start us, length us, event | category | flops | bytes accessed | tf_op | source)
XLA Modules:
  0.0 733.2 jit_solution(7389421801588177707)
XLA Ops:
  1.4 1.4 convert_reduce_fusion.1
  2.8 1.6 fusion.23
  5.7 111.1 %shard_map.220 = (bf16[1024,768]{1,0:T(8,128)(2,1)}, bf16[1024,1024]{1,0:T(8,128)(2,1)}, bf16[1024,1024]{1,0:T(8,128)(2,1)}, bf16[1024,1024]{1,0:T(8,128)(2,1)},...) custom-call(bf16[64,3072]{1,0:T(8,128)(2,1)} %wq.1, bf16[64,1024]{1,0:T(8,128)(2,1)} %wo.1, ...), custom_call_target="tpu_custom_call" | custom-call | tf_op jit(solution)/shard_map/pallas_call | solution.py:402
  117.8 3.0 convert_reduce_fusion
  121.2 1.4 fusion.7
  122.6 1.7 fusion.11
  124.3 1.9 copy-done.10
  126.3 4.7 convolution_convert_fusion.3.q.k.v
  131.0 10.7 %shard_map.221 = (bf16[2048,256]{1,0:T(8,128)(2,1)S(1)}, f32[2,2,1024,1]{3,2,1,0:T(8,128)S(1)}) custom-call(f32[2]{0:T(128)S(1)} %multiply_exponential_fusion.slopes, s32[2,3]{1,0:T(2,128)S(1)} %reduce_window_sum.11.ends, bf16[2048,768]{1,0:T(8,128)(2,1)} %convolution_convert_fusion.3.q.k.v, bf16[2048,768]{1,0:T(8,128)(2,1)} %convolution_convert_fusion.3.q.k.v, ...), custom_call_target="tpu_custom_call" | custom-call | tf_op jit(solution)/shard_map/pallas_call | solution.py:885
  142.7 1.3 copy-done.4
  144.0 34.6 %shard_map.222 = bf16[2048,1024]{1,0:T(8,128)(2,1)} custom-call(bf16[2048,256]{1,0:T(8,128)(2,1)} %copy-done.2), custom_call_target="tpu_custom_call" | custom-call | tf_op jit(solution)/shard_map/pallas_call | solution.py:402
  178.7 6.5 fusion.39
  186.9 1.6 copy-done.5
  188.6 1.7 add_convert_fusion
  190.3 4.6 fusion.40
  194.9 6.2 convolution_convert_fusion.5
  201.1 9.9 %fusion.33 = (f32[1024]{0:T(1024)S(1)}, bf16[2048,1024]{1,0:T(8,128)(2,1)S(1)}) fusion(f32[2048,1024]{1,0:T(8,128)S(1)} %fusion.40, f32[1024]{0:T(1024)S(1)} %bitcast.98, bf16[2048,1024]{1,0:T(8,128)(2,1)S(1)} %bitcast.103, bf16[1024,1024]{1,0:T(8,128)(2,1)S(1)} %copy-done.25), kind=kOutput, calls=%fused_computation.88 | convolution fusion | flops 4341103616 | bytes 18882560 | tf_op jit(solution)/shard_map/dot_general | solution.py:23
  211.1 7.0 convolution_convert_fusion.1
  218.0 6.2 fusion.27
  224.3 9.4 %convolution_convert_fusion.2 = bf16[2048,1024]{1,0:T(8,128)(2,1)} fusion(bf16[1024,1024]{1,0:T(8,128)(2,1)} %get-tuple-element.50, bf16[2048,1024]{1,0:T(8,128)(2,1)} %copy-done.28), kind=kOutput, calls=%fused_computation.27 | convolution fusion | flops 4297064448 | bytes 10485760 | tf_op jit(solution)/shard_map/dot_general | solution.py:23
  233.7 75.9 %shard_map.223 = (f32[512,1024]{1,0:T(8,128)}, f32[512,1024]{1,0:T(8,128)}, bf16[128,1024]{1,0:T(8,128)(2,1)}, bf16[128,1024]{1,0:T(8,128)(2,1)}) custom-call(bf16[4,512,1024]{2,1,0:T(8,128)(2,1)} %bitcast.85, bf16[4,512,1024]{2,1,0:T(8,128)(2,1)} %bitcast.84, bf16[8,128,1024]{2,1,0:T(8,128)(2,1)} %bitcast.90, bf16[8,128,1024]{2,1,0:T(8,128)(2,1)} %bitcast.91), custom_call_target="tpu_custom_call" | custom-call | tf_op jit(solution)/shard_map/pallas_call | solution.py:402
  309.6 3.3 multiply_reduce_fusion.1
  312.9 4.4 fusion.35
  317.3 35.4 %shard_map.224 = bf16[4,512,1024]{2,1,0:T(8,128)(2,1)} custom-call(bf16[512,1024]{1,0:T(8,128)(2,1)} %get-tuple-element.84.src), custom_call_target="tpu_custom_call" | custom-call | tf_op jit(solution)/shard_map/pallas_call | solution.py:402
  352.7 3.6 convolution_convert_fusion.4.do
  356.5 2.1 convolution_convert_fusion.7
  358.5 14.1 %shard_map.225 = (bf16[2048,256]{1,0:T(8,128)(2,1)S(1)}, bf16[2048,256]{1,0:T(8,128)(2,1)S(1)}, bf16[2048,256]{1,0:T(8,128)(2,1)S(1)}) custom-call(f32[2]{0:T(128)S(1)} %multiply_exponential_fusion.slopes, s32[2,3]{1,0:T(2,128)S(1)} %reduce_window_sum.11.ends, bf16[2048,768]{1,0:T(8,128)(2,1)} %convolution_convert_fusion.3.q.k.v, ...), custom_call_target="tpu_custom_call" | custom-call | tf_op jit(solution)/shard_map/pallas_call | solution.py:902
  372.9 1.9 copy-done.11
  374.8 4.7 convolution_convert_fusion.6
  379.5 5.1 convolution_convert_fusion
  384.7 42.8 %shard_map.226 = (f32[512,1024]{1,0:T(8,128)}, bf16[128,768]{1,0:T(8,128)(2,1)}, bf16[32,1024]{1,0:T(8,128)(2,1)}) custom-call(bf16[4,512,1024]{2,1,0:T(8,128)(2,1)} %bitcast.88, bf16[8,128,768]{2,1,0:T(8,128)(2,1)} %bitcast.92, bf16[8,32,1024]{2,1,0:T(8,128)(2,1)} %bitcast.93), custom_call_target="tpu_custom_call" | custom-call | tf_op jit(solution)/shard_map/pallas_call | solution.py:402
  427.5 2.7 fusion.22
  430.2 43.7 %psum.7 = f32[9216]{0:T(1024)S(1)} all-reduce(f32[9216]{0:T(1024)S(1)} %constant_dynamic-update-slice_fusion.4), channel_id=1, replica_groups=mesh['dp'=16,'seq'=2] {'dp','seq'}, use_global_device_ids=true, to_apply=%region_19.20 | all-reduce | flops 9216 | bytes 73728 | tf_op jit(solution)/shard_map/psum | solution.py:1021
  474.0 3.3 fusion.21
  480.4 133.3 %shard_map.227 = bf16[32,384,1024]{2,1,0:T(8,128)(2,1)} custom-call(bf16[384,1024]{1,0:T(8,128)(2,1)} %maximum_maximum_fusion.src), custom_call_target="tpu_custom_call" | custom-call | tf_op jit(solution)/shard_map/pallas_call | solution.py:402
  613.7 1.8 slice.83
  615.5 2.0 copy.36
  617.5 3.0 copy.45
  620.5 6.3 slice.82
  626.9 8.6 %copy.42 = bf16[8,4,1,128,768]{3,4,1,0,2:T(8,128)(2,1)} copy(bf16[8,4,1,128,768]{4,3,2,1,0:T(8,128)(2,1)} %slice.82) | data formatting | bytes 12582912
  635.5 10.0 %fusion.36 = (bf16[8,4,1,128,1024]{4,3,2,1,0:T(8,128)(2,1)}, f32[8,4,1,128,1024]{4,3,2,1,0:T(8,128)S(1)}) fusion(bf16[8,4,3,128,1024]{4,3,2,1,0:T(8,128)(2,1)} %bitcast.77), kind=kLoop, calls=%fused_computation.90 | loop fusion | flops 4194304 | bytes 41943040 | tf_op jit(solution)/shard_map/slice | solution.py:1001
  645.5 3.7 copy.46
  649.2 12.2 %copy.48 = f32[8,4,128,8,128]{4,1,3,2,0:T(4,128)} copy(f32[8,4,128,8,128]{4,3,2,1,0:T(8,128)S(1)} %bitcast.79) | data formatting | bytes 33554432 | tf_op jit(solution)/shard_map/convert_element_type | solution.py:1003
  661.4 19.9 %reshape.224 = f32[1024,4096]{1,0:T(8,128)} reshape(f32[8,128,8,4,128]{4,3,2,1,0:T(4,128)} %bitcast.80) | data formatting | bytes 33554432 | tf_op jit(solution)/shard_map/convert_element_type | solution.py:1003
  681.4 9.3 %convert_bitcast_fusion = f32[8,128,3,4,256]{1,4,2,3,0:T(8,128)} fusion(bf16[8,4,128,3,256]{2,4,3,1,0:T(8,128)(2,1)} %bitcast.81), kind=kLoop, calls=%fused_computation.1 | loop fusion | flops 3145728 | bytes 18874368 | tf_op jit(solution)/shard_map/convert_element_type | solution.py:1005
  690.7 14.6 %copy.40 = f32[8,128,3,4,256]{4,3,2,1,0:T(4,128)} copy(f32[8,128,3,4,256]{1,4,2,3,0:T(8,128)} %convert_bitcast_fusion) | data formatting | bytes 25165824
  705.2 15.9 %reshape.229 = f32[1024,3072]{1,0:T(8,128)} reshape(f32[8,128,3,4,256]{4,3,2,1,0:T(4,128)} %copy.40) | data formatting | bytes 25165824
  721.1 11.7 %bitcast_convert_fusion = f32[4096,1024]{1,0:T(8,128)} fusion(bf16[8,4,1,128,1024]{4,3,2,1,0:T(8,128)(2,1)} %get-tuple-element.86), kind=kLoop, calls=%fused_computation.11 | loop fusion | flops 4194304 | bytes 25165824 | tf_op jit(solution)/shard_map/convert_element_type | solution.py:1001
  (90 shorter events, 9.4 us)
Async XLA Ops:
  0.6 0.7 copy-start
  117.7 3.4 copy-start.6
  117.7 4.9 copy-start.17
  117.8 4.9 copy-start.19
  122.6 3.6 copy-start.26
  124.3 1.9 copy-start.10
  141.8 1.0 copy-start.2
  142.7 1.3 copy-start.4
  144.0 34.6 %copy-start.23 = (bf16[1024,1024]{1,0:T(8,128)(2,1)S(1)}, bf16[1024,1024]{1,0:T(8,128)(2,1)}, u32[]{:S(2)}) copy-start(bf16[1024,1024]{1,0:T(8,128)(2,1)} %get-tuple-element.47) | copy-start | bytes 6291460
  185.2 3.4 copy-start.5
  185.7 2.8 copy-start.18
  185.7 2.8 copy-start.20
  188.6 1.7 copy-start.24
  190.3 4.6 copy-start.22
  194.9 6.2 copy-start.25
  211.0 7.0 copy-start.28
  309.6 3.3 copy-start.9
  309.6 3.3 copy-start.13
  309.6 3.3 copy-start.21
  352.7 3.7 copy-start.3
  352.7 3.8 copy-start.12
  372.6 2.2 copy-start.11
  374.8 4.7 copy-start.27
  384.7 42.8 %copy-start.7 = (bf16[512,1024]{1,0:T(8,128)(2,1)S(1)}, bf16[512,1024]{1,0:T(8,128)(2,1)}, u32[]{:S(2)}) copy-start(bf16[512,1024]{1,0:T(8,128)(2,1)} %tok.1) | copy-start | bytes 3145732
  427.5 46.6 %copy-start.8 = (f32[512,1024]{1,0:T(8,128)S(1)}, f32[512,1024]{1,0:T(8,128)}, u32[]{:S(2)}) copy-start(f32[512,1024]{1,0:T(8,128)} %get-tuple-element.57) | copy-start | bytes 6291460
  427.5 51.9 %copy-start.14 = (bf16[128,1024]{1,0:T(8,128)(2,1)S(1)}, bf16[128,1024]{1,0:T(8,128)(2,1)}, u32[]{:S(2)}) copy-start(bf16[128,1024]{1,0:T(8,128)(2,1)} %get-tuple-element.58) | copy-start | bytes 786436
  474.0 5.4 copy-start.15
  474.0 5.4 copy-start.16
  721.1 11.7 %copy-start.1 = (f32[4096]{0:T(1024)S(1)}, f32[4096]{0:T(1024)}, u32[]{:S(2)}) copy-start(f32[4096]{0:T(1024)} %param.24) | copy-start | bytes 49156
